TPU v7x, 32 devices: a whole 2x2x4 slice. The times are simulated.
32 devices in a mesh: ex: 8 (over z, x), ey: 4 (over y, core).
Axes of the slice: x: 2, y: 2, z: 4, core: 2. Of those that a mesh axis runs over, the one named last changes fastest.
Arguments:
- weights: bfloat16 [32, 7168, 1536], P(('ex', 'ey')), may hold values from -6 to 6
- fisher: float32 [32, 7168], P(('ex', 'ey')), may hold values from 0.3 to 3
- start: bfloat16 [7168, 128], P(('ex', 'ey')), may hold values from -6 to 6
Outputs:
- basis: float32 [7168, 128], P(('ex', 'ey'))
- coeffs: bfloat16 [32, 128, 1536], P(('ex', 'ey'))
All inputs are finite; a program needn't handle non-finite values.
Results may differ from a plain program's by a relative error of at most 0.0054.
Values may be sent and summed in bfloat16 or wider, within the bound.
A program may use at most 128 MiB of HBM per device.

v0:
```python
import jax
import jax.numpy as jnp
from jax import lax
from jax.sharding import PartitionSpec as P


def body(weights, fisher, start):
    matrix = weights[0]
    row_weight = fisher[0]
    width = matrix.shape[0]
    rows = matrix
    scale = row_weight
    weighted = (
        scale[:, None] * lax.all_gather(start, ("ex", "ey"), axis=0, tiled=True).astype(jnp.float32)
    ).astype(jnp.bfloat16)
    projected = lax.dot_general(
        rows, weighted, (((0,), (0,)), ((), ())), preferred_element_type=jnp.float32
    ).astype(jnp.bfloat16)
    rows = matrix
    scale = row_weight
    sketch_part = lax.psum_scatter(
        jnp.dot(rows, projected, preferred_element_type=jnp.float32) * scale[:, None],
        ("ex", "ey"),
        scatter_dimension=0,
        tiled=True,
    )
    partial_gram = jnp.dot(sketch_part.T, sketch_part, precision=lax.Precision.HIGHEST)
    gram = lax.psum(partial_gram, ("ex", "ey"))
    lower = jnp.linalg.cholesky(gram)
    ortho_part = lax.linalg.triangular_solve(
        lower, sketch_part, left_side=False, lower=True, transpose_a=True
    )
    rows = matrix
    scale = row_weight
    scaled = (scale[:, None] * lax.all_gather(ortho_part, ("ex", "ey"), axis=0, tiled=True)).astype(
        jnp.bfloat16
    )
    coeff_sum = lax.dot_general(
        scaled, rows, (((0,), (0,)), ((), ())), preferred_element_type=jnp.float32
    )
    basis = ortho_part * jnp.sqrt(jnp.float32(width))
    coeffs = coeff_sum.astype(jnp.bfloat16)[None]
    return (basis, coeffs)


def solution(mesh):
    placed = (P(("ex", "ey"), None, None), P(("ex", "ey"), None), P(("ex", "ey"), None))
    return jax.shard_map(
        body,
        mesh=mesh,
        in_specs=placed,
        out_specs=(P(("ex", "ey"), None), P(("ex", "ey"), None, None)),
        check_vma=False,
    )
```

profile of v0, /device:TPU:0, one launch (start us, length us, event | category | flops | bytes accessed | tf_op | source)
XLA Modules:
  0.0 465.7 jit_solution(6922824760273048100)
XLA Ops:
  7.2 0.0 all-gather.3.cloned.1.call-start
  7.2 0.7 all-gather.3.cloned.1.call-update
  7.9 0.0 reduce-scatter.4.cloned.1.call-start
  7.9 61.4 %all-gather.3.cloned.1.call-done = bf16[7168,128]{1,0:T(8,128)(2,1)} async-done(((bf16[224,128]{1,0:T(8,128)(2,1)}), bf16[7168,128]{1,0:T(8,128)(2,1)}) %all-gather.3.cloned.1.call-update) | async-done | bytes 1835024 | tf_op jit(solution)/shard_map/all_gather | solution.py:14
  69.4 0.0 copy-start
  69.4 11.1 %fusion.12.clone.4 = bf16[128,1536]{1,0:T(8,128)(2,1)S(1)} fusion(bf16[1,7168,1536]{2,1,0:T(8,128)(2,1)} %param.3, bf16[7168,128]{1,0:T(8,128)(2,1)} %all-gather.3.cloned.1.call-done, f32[7168]{0:T(1024)} %bitcast.45), kind=kOutput, calls=%fused_computation.10.clone.clone.clone.1 | convolution fusion | flops 2821521408 | bytes 24276992 | tf_op jit(solution)/shard_map/dot_general | solution.py:16
  80.5 0.0 copy-done
  80.5 13.6 %fusion.9 = f32[7168,128]{0,1:T(8,128)} fusion(bf16[1,7168,1536]{2,1,0:T(8,128)(2,1)} %param.3, f32[7168]{0:T(1024)S(1)} %bitcast.46, bf16[128,1536]{1,0:T(8,128)(2,1)S(1)} %fusion.12.clone.4), kind=kOutput, calls=%fused_computation.7 | convolution fusion | flops 2819489792 | bytes 26112000 | tf_op jit(solution)/shard_map/dot_general | solution.py:22
  94.0 5.3 %copy.10 = f32[7168,128]{1,0:T(8,128)} copy(f32[7168,128]{0,1:T(8,128)} %fusion.9) | data formatting | bytes 7340032
  99.3 0.0 reduce-scatter.4.cloned.1.call-update
  99.3 0.0 all-reduce.2.cloned.1.call-start
  99.4 139.0 %reduce-scatter.4.cloned.1.call-done = f32[224,128]{1,0:T(8,128)} async-done(((f32[7168,128]{1,0:T(8,128)}), f32[224,128]{1,0:T(8,128)}) %reduce-scatter.4.cloned.1.call-update) | async-done | bytes 114704
  238.3 2.0 fusion.30
  240.3 0.0 all-reduce.2.cloned.1.call-update
  240.4 0.2 all-gather.5.cloned.1.call-start
  240.6 118.3 %all-reduce.2.cloned.1.call-done = f32[128,128]{0,1:T(8,128)} async-done(((f32[128,128]{0,1:T(8,128)}), f32[128,128]{0,1:T(8,128)}) %all-reduce.2.cloned.1.call-update) | async-done | bytes 65552 | tf_op jit(solution)/shard_map/psum | solution.py:28
  358.9 0.9 copy.8
  359.9 0.9 fusion.29
  360.7 11.7 %cholesky.16 = f32[128,128]{1,0:T(8,128)S(1)} custom-call(f32[128,128]{1,0:T(8,128)S(1)} %fusion.29), custom_call_target="Cholesky" | custom-call | tf_op jit(solution)/shard_map/jit(cholesky)/cholesky | solution.py:29
  372.5 0.6 compare_reduce_fusion
  373.1 0.7 fusion.26
  373.8 9.8 %custom-call.6 = f32[1,128,128]{1,2,0:T(8,128)S(1)} custom-call(f32[1,128,128]{2,1,0:T(8,128)S(1)} %fusion.26), custom_call_target="InvertDiagBlocksLowerTriangular" | custom-call | tf_op jit(solution)/shard_map/triangular_solve | solution.py:30
  383.6 1.8 broadcast_multiply_fusion
  385.4 0.0 all-gather.5.cloned.1.call-update
  385.4 61.3 %all-gather.5.cloned.1.call-done = f32[7168,128]{1,0:T(8,128)} async-done(((f32[224,128]{1,0:T(8,128)}), f32[7168,128]{1,0:T(8,128)}) %all-gather.5.cloned.1.call-update) | async-done | bytes 3670032 | tf_op jit(solution)/shard_map/all_gather | solution.py:35
  446.8 12.4 %fusion.20 = bf16[1,128,1536]{2,1,0:T(8,128)(2,1)} fusion(bf16[1,7168,1536]{2,1,0:T(8,128)(2,1)} %param.3, f32[7168,128]{1,0:T(8,128)} %all-gather.5.cloned.1.call-done, f32[7168]{0:T(1024)S(1)} %bitcast.47), kind=kOutput, calls=%fused_computation.12 | convolution fusion | flops 2820603904 | bytes 26112000 | tf_op jit(solution)/shard_map/dot_general | solution.py:38
  (1 shorter events, 0.0 us)
Async XLA Ops:
  7.2 62.2 %all-gather.3.cloned.1.call-start = ((), (), s32[]{:S(2)}) async-start(), calls=%async_computation.1 | async-start | bytes 1892352 | tf_op jit(solution)/shard_map/all_gather | solution.py:14
  7.9 230.4 %reduce-scatter.4.cloned.1.call-start = ((), (), s32[]{:S(2)}) async-start(), calls=%async_computation.4 | async-start | bytes 3784704
  69.4 11.1 %copy-start = (f32[1,7168]{1,0:T(1,128)S(1)}, f32[1,7168]{1,0:T(1,128)}, u32[]{:S(2)}) copy-start(f32[1,7168]{1,0:T(1,128)} %param.4) | copy-start | bytes 86020
  99.3 259.6 %all-reduce.2.cloned.1.call-start = ((), (), s32[]{:S(2)}) async-start(), calls=%async_computation.2 | async-start | bytes 131072 | tf_op jit(solution)/shard_map/psum | solution.py:28
  240.4 206.4 %all-gather.5.cloned.1.call-start = ((), (), s32[]{:S(2)}) async-start(), calls=%async_computation.3 | async-start | bytes 3784704 | tf_op jit(solution)/shard_map/all_gather | solution.py:35
Sparse Core Ops, SparseCore 0:
  10.9 58.4 all-gather.2
  99.4 138.8 reduce-scatter.3
  245.4 113.4 all-reduce.1
  385.6 61.1 all-gather.4
where the time goes:
time: 466 us
  waiting for transfers between devices  381 us (82%)
  matrix products  40.9 us (9%)
  other arithmetic  23.7 us (5%)
  between operations  13.8 us (3%)
  local copies, waits for them, and re-layouts  6.19 us (1%)
    unnamed x5, waiting for transfers between devices  140 us
    psum x1, waiting for transfers between devices, body(): gram = lax.psum(partial_gram, ('ex', 'ey'))  118 us
    all_gather x1, waiting for transfers between devices, body(): lax.all_gather(start, ('ex', 'ey'), axis=0, tiled=True).astype(jnp.float32)  61.4 us
    all_gather x1, waiting for transfers between devices, body(): lax.all_gather(ortho_part, ('ex', 'ey'), axis=0, tiled=True)  61.3 us
    dot_general x1, matrix products, body(): jnp.dot(rows, projected, preferred_element_type=jnp.float32)  13.6 us
    another operation x3, other arithmetic, body(): lower = jnp.linalg.cholesky(gram)  12.4 us
    dot_general x1, matrix products, body(): lax.dot_general(scaled, rows, (((0,), (0,)), ((), ())), preferred_element...  12.4 us
    dot_general x1, matrix products, body(): lax.dot_general(rows, weighted, (((0,), (0,)), ((), ())), preferred_eleme...  11.1 us
  transfers between devices with their start and end apart: 4, of which 4 were waited for; matrix products, arithmetic and copies ran while one was open for 0% of the time, Pallas kernels for 0%

commit v1 on v0

v1 whole, which is shorter than its diff:
```python
import functools
import math

import jax
import jax.numpy as jnp
from jax import lax
from jax.experimental import pallas as pl
from jax.experimental.pallas import tpu as pltpu
from jax.sharding import PartitionSpec as P

MESH = pl.DeviceIdType.MESH
BF16 = jnp.bfloat16
F32 = jnp.float32
HIGHEST = lax.Precision.HIGHEST
PANEL = 16


def power_kernel(
    Z,
    w_hbm, fisher_ref, start_ref,
    sketch_ref, gram_ref, raw_ref,
    w, fcol, starts, sketches, term, proj,
    core_out, core_in, one_out, one_in, two_out, two_in, z_out, z_in,
    w_sem, send_sem, recv_sem,
):
    ex, ey = lax.axis_index("ex"), lax.axis_index("ey")
    z, x, y, c = ex // 2, ex % 2, ey // 2, ey % 2
    rows, rank = start_ref.shape
    half = rows // 2
    chunk = 8 * rows
    width = w.shape[1]

    def z_of(k):
        low = (z % 2 + k % 2) % 2
        high = (z // 2 + k // 2) % 2
        return high * 2 + low

    z_peer = {k: (z_of(k) * 2 + x, ey) for k in range(1, Z)}
    x_peer = (z * 2 + (1 - x), ey)
    y_peer = (ex, (1 - y) * 2 + c)
    c_peer = (ex, y * 2 + (1 - c))

    def w_copy(k):
        at = pl.ds(pl.multiple_of(z_of(k) * chunk, chunk), chunk)
        return pltpu.make_async_copy(w_hbm.at[at], w.at[at], w_sem.at[k])

    for k in range(Z):
        w_copy(k).start()

    barrier = pltpu.get_barrier_semaphore()
    peers = [*z_peer.values(), x_peer, y_peer, c_peer]
    for peer in peers:
        pl.semaphore_signal(barrier, inc=1, device_id=peer, device_id_type=MESH)
    starts[z, x, y, c] = start_ref[...]
    pl.semaphore_wait(barrier, len(peers))

    copies = {}

    def send(key, src, dst, peer):
        i = len(copies)
        copies[key] = pltpu.make_async_remote_copy(
            src_ref=src, dst_ref=dst, send_sem=send_sem.at[i], recv_sem=recv_sem.at[i],
            device_id=peer, device_id_type=MESH,
        )
        copies[key].start()

    low, high = pl.ds(0, half), pl.ds(half, half)

    def gather(name, buf, ready, work=None):
        for k in range(1, Z):
            send((name, "z", k), buf.at[z, x, y, c], buf.at[z, x, y, c], z_peer[k])

        def first(k):
            if k > 0:
                copies[name, "z", k].wait_recv()
            a, b = buf.at[z_of(k), x, y, c, low], buf.at[z_of(k), x, y, c, high]
            send((name, 1, 0, k), a, a, x_peer)
            send((name, 1, 1, k), b, b, y_peer)

        def second(k):
            copies[name, 1, 0, k].wait_recv()
            a = buf.at[z_of(k), :, y, c, low]
            send((name, 2, 0, k), a, a, y_peer)
            copies[name, 1, 1, k].wait_recv()
            b = buf.at[z_of(k), x, :, c, high]
            send((name, 2, 1, k), b, b, x_peer)

        def third(k):
            copies[name, 2, 0, k].wait_recv()
            copies[name, 2, 1, k].wait_recv()
            a = buf.at[z_of(k), :, :, c]
            send((name, 3, k), a, a, c_peer)

        def fourth(k):
            copies[name, 3, k].wait_recv()
            ready(k)

        for t in range(Z + 3):
            for stage, f in enumerate((first, second, third)):
                if 0 <= t - stage < Z:
                    f(t - stage)
            if work is not None and t == 0:
                work()
            if 0 <= t - 3 < Z:
                fourth(t - 3)

    def w_rows(k):
        return w.at[pl.ds(pl.multiple_of(z_of(k) * chunk, chunk), chunk)]

    def turned(buf, k):
        return buf[z_of(k)].reshape(chunk, rank).astype(F32).T

    def add_product(out, left, k):
        matrix = w_rows(k)
        tile = 512
        for n in range(width // tile):
            at = slice(n * tile, (n + 1) * tile)
            part = jnp.dot(left, matrix[:, at], preferred_element_type=F32)
            out[:, at] = part if k == 0 else out[:, at] + part

    def columns():
        for q in range(Z):
            fcol[q] = jnp.broadcast_to(fisher_ref[q], (rank, chunk)).T

    def project(k):
        left = (turned(starts, k) * fisher_ref[z_of(k)]).astype(BF16)
        w_copy(k).wait()
        add_product(raw_ref, left, k)

    gather("start", starts, project, columns)
    proj[...] = raw_ref[...].T.astype(BF16)

    def compute(k):
        q = z_of(k)

        def pair(i, carry):
            at = pl.ds(pl.multiple_of(q * chunk + i * 2 * rows, 2 * rows), 2 * rows)
            part = jnp.dot(w[at], proj[...], preferred_element_type=F32)
            inner = pl.ds(pl.multiple_of(i * 2 * rows, 2 * rows), 2 * rows)
            part = part * fcol[q, inner]
            term[q, i // 2, i % 2] = part.reshape(2, rows, rank)
            core_out[k, i // 2, i % 2] = term[q, i // 2, i % 2, 1 - c].astype(BF16)
            return carry

        lax.fori_loop(0, 4, pair, 0)
        send(("sum", 0, k), core_out.at[k], core_in.at[k], c_peer)

    def sum_core(k):
        q = z_of(k)
        copies["sum", 0, k].wait_recv()
        for i in range(2):
            for j in range(2):
                term[q, i, j, c] = term[q, i, j, c] + core_in[k, i, j].astype(F32)
        for i in range(2):
            one_out[0, k, i] = term[q, i, 1 - y, c, low].astype(BF16)
            one_out[1, k, i] = term[q, 1 - x, i, c, high].astype(BF16)
        send(("sum", 1, 0, k), one_out.at[0, k], one_in.at[0, k], y_peer)
        send(("sum", 1, 1, k), one_out.at[1, k], one_in.at[1, k], x_peer)

    def sum_one(k):
        q = z_of(k)
        copies["sum", 1, 0, k].wait_recv()
        two_out[0, k] = (term[q, 1 - x, y, c, low] + one_in[0, k, 1 - x].astype(F32)).astype(BF16)
        send(("sum", 2, 0, k), two_out.at[0, k], two_in.at[0, k], x_peer)
        copies["sum", 1, 1, k].wait_recv()
        two_out[1, k] = (term[q, x, 1 - y, c, high] + one_in[1, k, 1 - y].astype(F32)).astype(BF16)
        send(("sum", 2, 1, k), two_out.at[1, k], two_in.at[1, k], y_peer)

    def sum_two(k):
        q = z_of(k)
        copies["sum", 2, 0, k].wait_recv()
        copies["sum", 2, 1, k].wait_recv()
        top = term[q, x, y, c, low] + one_in[0, k, x].astype(F32) + two_in[0, k].astype(F32)
        bottom = term[q, x, y, c, high] + one_in[1, k, y].astype(F32) + two_in[1, k].astype(F32)
        if k > 0:
            z_out[k, low] = top.astype(BF16)
            z_out[k, high] = bottom.astype(BF16)
            send(("sum", 3, k), z_out.at[k], z_in.at[k], z_peer[k])
        else:
            sketch_ref[low] = top
            sketch_ref[high] = bottom

    order = list(range(Z))[::-1]
    for t in range(Z + 3):
        for stage, f in enumerate((compute, sum_core, sum_one, sum_two)):
            if 0 <= t - stage < Z:
                f(order[t - stage])
    total = sketch_ref[...]
    for k in order[:-1]:
        copies["sum", 3, k].wait_recv()
        total = total + z_in[k].astype(F32)
    sketch_ref[...] = total
    sketches[z, x, y, c] = total.astype(BF16)

    def finish(k):
        plain = turned(sketches, k)
        part = jnp.dot(
            plain.astype(BF16), sketches[z_of(k)].reshape(chunk, rank), preferred_element_type=F32
        )
        gram_ref[...] = part if k == 0 else gram_ref[...] + part
        add_product(raw_ref, (plain * fisher_ref[z_of(k)]).astype(BF16), k)

    gather("sketch", sketches, finish)
    for copy in copies.values():
        copy.wait_send()


def basis_kernel(scale, sketch_ref, gram_ref, raw_ref, basis_ref, coeffs_ref, work):
    n = gram_ref.shape[0]
    work[:, :n] = gram_ref[...]
    i0 = lax.broadcasted_iota(jnp.int32, (n, n), 0)
    i1 = lax.broadcasted_iota(jnp.int32, (n, n), 1)
    work[:, n:] = jnp.where(i0 == i1, 1.0, 0.0).astype(F32)
    line = lax.broadcasted_iota(jnp.int32, (PANEL, 1), 0)
    for p in range(n // PANEL):
        base = p * PANEL
        panel = work[base : base + PANEL, :]
        for j in range(PANEL):
            column = panel[:, base + j : base + j + 1]
            r = lax.rsqrt(panel[j : j + 1, base + j : base + j + 1])
            row = panel[j : j + 1, :] * r
            factor = jnp.where(line > j, column * r, 0.0)
            panel = jnp.where(line == j, row, panel - factor * row)
        work[base : base + PANEL, :] = panel
        end = base + PANEL
        if end < n:
            update = lax.dot_general(
                panel[:, :n], panel, (((0,), (0,)), ((), ())), precision=HIGHEST, preferred_element_type=F32
            )
            work[end:, :] = work[end:, :] - update[end:, :]
    inverse = work[:, n:]
    basis_ref[...] = scale * lax.dot_general(
        sketch_ref[...], inverse, (((1,), (1,)), ((), ())), precision=HIGHEST, preferred_element_type=F32
    )
    coeffs_ref[...] = jnp.dot(
        inverse, raw_ref[...], precision=HIGHEST, preferred_element_type=F32
    ).astype(BF16)


def fused_body(Z, weights, fisher, start):
    matrix = weights[0]
    depth, width = matrix.shape
    rows, rank = start.shape
    half, chunk = rows // 2, 8 * rows
    vmem = pl.BlockSpec(memory_space=pltpu.VMEM)
    n_copies = 3 * (Z - 1 + 5 * Z)
    sketch, gram, raw = pl.pallas_call(
        functools.partial(power_kernel, Z),
        out_shape=(
            jax.ShapeDtypeStruct((rows, rank), F32),
            jax.ShapeDtypeStruct((rank, rank), F32),
            jax.ShapeDtypeStruct((rank, width), F32),
        ),
        in_specs=[pl.BlockSpec(memory_space=pl.ANY), vmem, vmem],
        out_specs=(vmem, vmem, vmem),
        scratch_shapes=[
            pltpu.VMEM((depth, width), BF16),
            pltpu.VMEM((Z, chunk, rank), F32),
            pltpu.VMEM((Z, 2, 2, 2, rows, rank), BF16),
            pltpu.VMEM((Z, 2, 2, 2, rows, rank), BF16),
            pltpu.VMEM((Z, 2, 2, 2, rows, rank), F32),
            pltpu.VMEM((width, rank), BF16),
            pltpu.VMEM((Z, 2, 2, rows, rank), BF16),
            pltpu.VMEM((Z, 2, 2, rows, rank), BF16),
            pltpu.VMEM((2, Z, 2, half, rank), BF16),
            pltpu.VMEM((2, Z, 2, half, rank), BF16),
            pltpu.VMEM((2, Z, half, rank), BF16),
            pltpu.VMEM((2, Z, half, rank), BF16),
            pltpu.VMEM((Z, rows, rank), BF16),
            pltpu.VMEM((Z, rows, rank), BF16),
            pltpu.SemaphoreType.DMA((Z,)),
            pltpu.SemaphoreType.DMA((n_copies,)),
            pltpu.SemaphoreType.DMA((n_copies,)),
        ],
        compiler_params=pltpu.CompilerParams(
            collective_id=0, has_side_effects=True, vmem_limit_bytes=56 * 2**20
        ),
        cost_estimate=pl.CostEstimate(
            flops=6 * depth * width * rank, bytes_accessed=2 * depth * width, transcendentals=0
        ),
    )(matrix, fisher.reshape(Z, 1, chunk), start)
    basis, coeffs = pl.pallas_call(
        functools.partial(basis_kernel, math.sqrt(depth)),
        out_shape=(
            jax.ShapeDtypeStruct((rows, rank), F32),
            jax.ShapeDtypeStruct((rank, width), BF16),
        ),
        in_specs=[vmem, vmem, vmem],
        out_specs=(vmem, vmem),
        scratch_shapes=[pltpu.VMEM((rank, 2 * rank), F32)],
        compiler_params=pltpu.CompilerParams(vmem_limit_bytes=32 * 2**20),
    )(sketch, gram, raw)
    return basis, coeffs[None]


def plain_body(weights, fisher, start):
    axes = ("ex", "ey")
    matrix, scale = weights[0], fisher[0][:, None]
    width = matrix.shape[0]
    whole = lax.all_gather(start, axes, axis=0, tiled=True).astype(F32)
    projected = lax.dot_general(
        matrix, (scale * whole).astype(BF16), (((0,), (0,)), ((), ())), preferred_element_type=F32
    ).astype(BF16)
    term = jnp.dot(matrix, projected, preferred_element_type=F32) * scale
    sketch = lax.psum_scatter(term, axes, scatter_dimension=0, tiled=True)
    gram = lax.psum(jnp.dot(sketch.T, sketch, precision=HIGHEST), axes)
    lower = jnp.linalg.cholesky(gram)
    ortho = lax.linalg.triangular_solve(lower, sketch, left_side=False, lower=True, transpose_a=True)
    scaled = (scale * lax.all_gather(ortho, axes, axis=0, tiled=True)).astype(BF16)
    coeffs = lax.dot_general(scaled, matrix, (((0,), (0,)), ((), ())), preferred_element_type=F32)
    return ortho * jnp.sqrt(jnp.float32(width)), coeffs.astype(BF16)[None]


def solution(mesh):
    placed = (P(("ex", "ey"), None, None), P(("ex", "ey"), None), P(("ex", "ey"), None))
    if mesh.shape["ex"] == 8 and mesh.shape["ey"] == 4:
        body = functools.partial(fused_body, mesh.shape["ex"] // 2)
    else:
        body = plain_body
    return jax.shard_map(
        body,
        mesh=mesh,
        in_specs=placed,
        out_specs=(P(("ex", "ey"), None), P(("ex", "ey"), None, None)),
        check_vma=False,
    )
```

time: 466 us -> 79.4 us (0.17)
  waiting for transfers between devices: 381 us -> 0 us
  Pallas kernels: 0 us -> 75.5 us
  matrix products: 40.9 us -> 0 us
  other arithmetic: 23.7 us -> 0 us
  between operations: 13.8 us -> 0.65 us
    unnamed x5 -> x0, waiting for transfers between devices: 140 us -> none
    all_gather x2 -> x0, waiting for transfers between devices: 123 us -> none  [the longest x1 61.4 us: body(): lax.all_gather(start, ('ex', 'ey'), axis=0, tiled=True).astype(jnp.float32)]
    psum x1 -> x0, waiting for transfers between devices: 118 us -> none  [body(): gram = lax.psum(partial_gram, ('ex', 'ey'))]
    pallas_call x0 -> x2, Pallas kernels: none -> 75.5 us  [the longest x1 61 us: fused_body(): pl.pallas_call(functools.partial(power_kernel, Z), out_shape=(jax.ShapeDt...]
    dot_general x4 -> x0, matrix products: 39 us -> none  [the longest x1 13.6 us: body(): jnp.dot(rows, projected, preferred_element_type=jnp.float32)]
    another operation x5 -> x0, other arithmetic: 22.9 us -> none  [the longest x3 12.4 us: body(): lower = jnp.linalg.cholesky(gram)]
  transfers between devices with their start and end apart: 4 -> 0, of which waited for: 4 -> 0; matrix products, arithmetic and copies ran while one was open for 0% -> 0% of each run, Pallas kernels for 0% -> 0%
where the time goes in v1:
time: 79.4 us; the launch traced here: 79 us
  Pallas kernels  75.5 us (95%)
  local copies, waits for them, and re-layouts  2.86 us (4%)
    pallas_call x1, Pallas kernels, fused_body(): pl.pallas_call(functools.partial(power_kernel, Z), out_shape=(jax.ShapeDt...  61 us
    pallas_call x1, Pallas kernels, fused_body(): pl.pallas_call(functools.partial(basis_kernel, math.sqrt(depth)), out_sha...  14.6 us
    unnamed x6, local copies, waits for them, and re-layouts  2.86 us

profile of v1, /device:TPU:0, one launch (start us, length us, event | category | flops | bytes accessed | tf_op | source)
XLA Modules:
  0.0 79.0 jit_solution(11922063118950186211)
XLA Ops:
  0.6 61.0 %shard_map.50 = (f32[224,128]{1,0:T(8,128)}, f32[128,128]{1,0:T(8,128)}, f32[128,1536]{1,0:T(8,128)}) custom-call(bf16[7168,1536]{1,0:T(8,128)(2,1)} %bitcast.3, f32[4,1,1792]{2,1,0:T(1,128)} %bitcast.5, bf16[224,128]{1,0:T(8,128)(2,1)} %start_ref.1), custom_call_target="tpu_custom_call" | custom-call | flops 8455716864 | bytes 22020096 | tf_op jit(solution)/shard_map/pallas_call | solution.py:247
  61.6 0.0 copy-start
  61.6 1.1 %copy-done = f32[128,1536]{1,0:T(8,128)S(1)} copy-done((f32[128,1536]{1,0:T(8,128)S(1)}, f32[128,1536]{1,0:T(8,128)}, u32[]{:S(2)}) %copy-start) | copy-done | bytes 786456
  62.7 0.0 copy-start.1
  62.7 0.9 %copy-done.1 = f32[224,128]{1,0:T(8,128)S(1)} copy-done((f32[224,128]{1,0:T(8,128)S(1)}, f32[224,128]{1,0:T(8,128)}, u32[]{:S(2)}) %copy-start.1) | copy-done | bytes 114712
  63.6 0.0 copy-start.2
  63.6 0.8 %copy-done.2 = f32[128,128]{1,0:T(8,128)S(1)} copy-done((f32[128,128]{1,0:T(8,128)S(1)}, f32[128,128]{1,0:T(8,128)}, u32[]{:S(2)}) %copy-start.2) | copy-done | bytes 65560
  64.5 14.6 %shard_map.51 = (f32[224,128]{1,0:T(8,128)}, bf16[128,1536]{1,0:T(8,128)(2,1)}) custom-call(f32[224,128]{1,0:T(8,128)S(1)} %copy-done.1, f32[128,128]{1,0:T(8,128)S(1)} %copy-done.2, f32[128,1536]{1,0:T(8,128)S(1)} %copy-done), custom_call_target="tpu_custom_call" | custom-call | tf_op jit(solution)/shard_map/pallas_call | solution.py:282
Async XLA Ops:
  61.6 1.1 %copy-start = (f32[128,1536]{1,0:T(8,128)S(1)}, f32[128,1536]{1,0:T(8,128)}, u32[]{:S(2)}) copy-start(f32[128,1536]{1,0:T(8,128)} %get-tuple-element.9.raw_ref) | copy-start | bytes 2359300
  62.7 0.9 %copy-start.1 = (f32[224,128]{1,0:T(8,128)S(1)}, f32[224,128]{1,0:T(8,128)}, u32[]{:S(2)}) copy-start(f32[224,128]{1,0:T(8,128)} %get-tuple-element.7.sketch_ref) | copy-start | bytes 344068
  63.6 0.8 %copy-start.2 = (f32[128,128]{1,0:T(8,128)S(1)}, f32[128,128]{1,0:T(8,128)}, u32[]{:S(2)}) copy-start(f32[128,128]{1,0:T(8,128)} %get-tuple-element.8.gram_ref) | copy-start | bytes 196612

commit v2 on v1

--- a/solution.py
+++ b/solution.py
@@ -13,12 +13,14 @@
 F32 = jnp.float32
 HIGHEST = lax.Precision.HIGHEST
 PANEL = 16
+GROUP = 4
 
 
 def power_kernel(
     Z,
     w_hbm, fisher_ref, start_ref,
-    sketch_ref, gram_ref, raw_ref,
+    basis_ref, coeffs_ref,
+    sketch_ref, gram_ref, raw_ref, work,
     w, fcol, starts, sketches, term, proj,
     core_out, core_in, one_out, one_in, two_out, two_in, z_out, z_in,
     w_sem, send_sem, recv_sem,
@@ -130,19 +132,21 @@
     gather("start", starts, project, columns)
     proj[...] = raw_ref[...].T.astype(BF16)
 
-    def compute(k):
+    def compute(k, between):
         q = z_of(k)
 
-        def pair(i, carry):
+        def pair(i):
             at = pl.ds(pl.multiple_of(q * chunk + i * 2 * rows, 2 * rows), 2 * rows)
             part = jnp.dot(w[at], proj[...], preferred_element_type=F32)
-            inner = pl.ds(pl.multiple_of(i * 2 * rows, 2 * rows), 2 * rows)
+            inner = pl.ds(i * 2 * rows, 2 * rows)
             part = part * fcol[q, inner]
             term[q, i // 2, i % 2] = part.reshape(2, rows, rank)
             core_out[k, i // 2, i % 2] = term[q, i // 2, i % 2, 1 - c].astype(BF16)
-            return carry
-
-        lax.fori_loop(0, 4, pair, 0)
+
+        for i in range(4):
+            pair(i)
+            if i < 3:
+                between[i]()
         send(("sum", 0, k), core_out.at[k], core_in.at[k], c_peer)
 
     def sum_core(k):
@@ -182,9 +186,15 @@
 
     order = list(range(Z))[::-1]
     for t in range(Z + 3):
-        for stage, f in enumerate((compute, sum_core, sum_one, sum_two)):
-            if 0 <= t - stage < Z:
-                f(order[t - stage])
+        between = [
+            functools.partial(f, order[t - stage]) if 0 <= t - stage < Z else lambda: None
+            for stage, f in enumerate((sum_core, sum_one, sum_two), 1)
+        ]
+        if t < Z:
+            compute(order[t], between)
+        else:
+            for f in between:
+                f()
     total = sketch_ref[...]
     for k in order[:-1]:
         copies["sum", 3, k].wait_recv()
@@ -201,26 +211,50 @@
         add_product(raw_ref, (plain * fisher_ref[z_of(k)]).astype(BF16), k)
 
     gather("sketch", sketches, finish)
+    finish_basis(math.sqrt(Z * chunk), sketch_ref, gram_ref, raw_ref, basis_ref, coeffs_ref, work)
     for copy in copies.values():
         copy.wait_send()
 
 
-def basis_kernel(scale, sketch_ref, gram_ref, raw_ref, basis_ref, coeffs_ref, work):
+def finish_basis(scale, sketch_ref, gram_ref, raw_ref, basis_ref, coeffs_ref, work):
     n = gram_ref.shape[0]
     work[:, :n] = gram_ref[...]
     i0 = lax.broadcasted_iota(jnp.int32, (n, n), 0)
     i1 = lax.broadcasted_iota(jnp.int32, (n, n), 1)
     work[:, n:] = jnp.where(i0 == i1, 1.0, 0.0).astype(F32)
-    line = lax.broadcasted_iota(jnp.int32, (PANEL, 1), 0)
+    line = lax.broadcasted_iota(jnp.int32, (PANEL, n), 0)
+
+    def spread(a):
+        return jnp.broadcast_to(a, (PANEL, n))
+
     for p in range(n // PANEL):
         base = p * PANEL
-        panel = work[base : base + PANEL, :]
-        for j in range(PANEL):
-            column = panel[:, base + j : base + j + 1]
-            r = lax.rsqrt(panel[j : j + 1, base + j : base + j + 1])
-            row = panel[j : j + 1, :] * r
-            factor = jnp.where(line > j, column * r, 0.0)
-            panel = jnp.where(line == j, row, panel - factor * row)
+        left, right = work[base : base + PANEL, :n], work[base : base + PANEL, n:]
+        for j in range(0, PANEL, GROUP):
+            group = range(GROUP)
+            lrow = [spread(left[j + i : j + i + 1, :]) for i in group]
+            rrow = [spread(right[j + i : j + i + 1, :]) for i in group]
+            column = [spread(left[:, base + j + i : base + j + i + 1]) for i in group]
+            corner = {
+                (i, m): spread(left[j + i : j + i + 1, base + j + m : base + j + m + 1])
+                for i in group for m in group if m >= i
+            }
+            for i in group:
+                r = lax.rsqrt(corner[i, i])
+                lrow[i], rrow[i], column[i] = lrow[i] * r, rrow[i] * r, column[i] * r
+                for m in range(i + 1, GROUP):
+                    corner[i, m] = corner[i, m] * r
+                for m in range(i + 1, GROUP):
+                    f = corner[i, m]
+                    lrow[m], rrow[m] = lrow[m] - f * lrow[i], rrow[m] - f * rrow[i]
+                    column[m] = column[m] - f * column[i]
+                    for q in range(m, GROUP):
+                        corner[m, q] = corner[m, q] - f * corner[i, q]
+            for i in group:
+                f = jnp.where(line >= j + GROUP, column[i], 0.0)
+                left = jnp.where(line == j + i, lrow[i], left - f * lrow[i])
+                right = jnp.where(line == j + i, rrow[i], right - f * rrow[i])
+        panel = jnp.concatenate([left, right], axis=1)
         work[base : base + PANEL, :] = panel
         end = base + PANEL
         if end < n:
@@ -244,16 +278,19 @@
     half, chunk = rows // 2, 8 * rows
     vmem = pl.BlockSpec(memory_space=pltpu.VMEM)
     n_copies = 3 * (Z - 1 + 5 * Z)
-    sketch, gram, raw = pl.pallas_call(
+    basis, coeffs = pl.pallas_call(
         functools.partial(power_kernel, Z),
         out_shape=(
             jax.ShapeDtypeStruct((rows, rank), F32),
-            jax.ShapeDtypeStruct((rank, rank), F32),
-            jax.ShapeDtypeStruct((rank, width), F32),
+            jax.ShapeDtypeStruct((rank, width), BF16),
         ),
         in_specs=[pl.BlockSpec(memory_space=pl.ANY), vmem, vmem],
-        out_specs=(vmem, vmem, vmem),
+        out_specs=(vmem, vmem),
         scratch_shapes=[
+            pltpu.VMEM((rows, rank), F32),
+            pltpu.VMEM((rank, rank), F32),
+            pltpu.VMEM((rank, width), F32),
+            pltpu.VMEM((rank, 2 * rank), F32),
             pltpu.VMEM((depth, width), BF16),
             pltpu.VMEM((Z, chunk, rank), F32),
             pltpu.VMEM((Z, 2, 2, 2, rows, rank), BF16),
@@ -279,17 +316,6 @@
             flops=6 * depth * width * rank, bytes_accessed=2 * depth * width, transcendentals=0
         ),
     )(matrix, fisher.reshape(Z, 1, chunk), start)
-    basis, coeffs = pl.pallas_call(
-        functools.partial(basis_kernel, math.sqrt(depth)),
-        out_shape=(
-            jax.ShapeDtypeStruct((rows, rank), F32),
-            jax.ShapeDtypeStruct((rank, width), BF16),
-        ),
-        in_specs=[vmem, vmem, vmem],
-        out_specs=(vmem, vmem),
-        scratch_shapes=[pltpu.VMEM((rank, 2 * rank), F32)],
-        compiler_params=pltpu.CompilerParams(vmem_limit_bytes=32 * 2**20),
-    )(sketch, gram, raw)
     return basis, coeffs[None]
 
 

time: 79.4 us -> 73.2 us (0.922)
  Pallas kernels: 75.5 us -> 69 us
    pallas_call x1 -> x0, Pallas kernels: 14.6 us -> none  [fused_body(): pl.pallas_call(functools.partial(basis_kernel, math.sqrt(depth)), out_sha...]
    pallas_call x1, Pallas kernels: 61 us -> 69 us  [fused_body(): pl.pallas_call(functools.partial(power_kernel, Z), out_shape=(jax.ShapeDt...]
    unnamed x6 -> x2, local copies, waits for them, and re-layouts: 2.86 us -> 3.32 us
where the time goes in v2:
time: 73.2 us; the launch traced here: 73 us
  Pallas kernels  69 us (94%)
  local copies, waits for them, and re-layouts  3.32 us (5%)
    pallas_call x1, Pallas kernels, fused_body(): pl.pallas_call(functools.partial(power_kernel, Z), out_shape=(jax.ShapeDt...  69 us
    unnamed x2, local copies, waits for them, and re-layouts  3.32 us

profile of v2, /device:TPU:0, one launch (start us, length us, event | category | flops | bytes accessed | tf_op | source)
XLA Modules:
  0.0 73.0 jit_solution(2481176367990020583)
XLA Ops:
  0.6 69.0 %shard_map.50 = (f32[224,128]{1,0:T(8,128)}, bf16[128,1536]{1,0:T(8,128)(2,1)}) custom-call(bf16[7168,1536]{1,0:T(8,128)(2,1)} %bitcast.4, f32[4,1,1792]{2,1,0:T(1,128)} %bitcast.5, bf16[224,128]{1,0:T(8,128)(2,1)} %start_ref.1), custom_call_target="tpu_custom_call" | custom-call | flops 8455716864 | bytes 22020096 | tf_op jit(solution)/shard_map/pallas_call | solution.py:281
  69.7 1.6 %copy.7 = f32[224,128]{1,0:T(8,128)} copy(f32[224,128]{1,0:T(8,128)} %get-tuple-element.8) | data formatting | bytes 229376
  71.2 1.8 %copy.8 = bf16[1,128,1536]{2,1,0:T(8,128)(2,1)} copy(bf16[1,128,1536]{2,1,0:T(8,128)(2,1)} %bitcast.3) | data formatting | bytes 786432
